TPU v7x, 32 devices: a whole 2x2x4 slice. The times are simulated.
32 devices in a mesh: row: 8 (over z, x), col: 2 (over y), ch: 2 (over core).
Axes of the slice: x: 2, y: 2, z: 4, core: 2. Of those that a mesh axis runs over, the one named last changes fastest.
Arguments:
- pair: bfloat16 [192, 192, 128], P('row', 'col'), may hold values from -6 to 6
- cotangent: bfloat16 [192, 192, 128], P('row', 'col', 'ch'), may hold values from -6 to 6
- w_gate_a: bfloat16 [128, 128], P(None, 'ch'), may hold values from -0.5 to 0.5
- w_proj_a: bfloat16 [128, 128], P(None, 'ch'), may hold values from -0.5 to 0.5
- w_gate_b: bfloat16 [128, 128], P(None, 'ch'), may hold values from -0.5 to 0.5
- w_proj_b: bfloat16 [128, 128], P(None, 'ch'), may hold values from -0.5 to 0.5
- w_gate_out: bfloat16 [128, 128], P(None, 'ch'), may hold values from -0.5 to 0.5
- w_out: bfloat16 [128, 128], P(None, 'ch'), may hold values from -0.5 to 0.5
Outputs:
- updated: bfloat16 [192, 192, 128], P('row', 'col', 'ch')
- grad_pair: bfloat16 [192, 192, 128], P('row', 'col', 'ch')
- grad_gate_a: float32 [128, 128], P(None, 'ch')
- grad_proj_a: float32 [128, 128], P(None, 'ch')
- grad_gate_b: float32 [128, 128], P(None, 'ch')
- grad_proj_b: float32 [128, 128], P(None, 'ch')
- grad_gate_out: float32 [128, 128], P(None, 'ch')
- grad_out: float32 [128, 128], P(None, 'ch')
All inputs are finite; a program needn't handle non-finite values.
Results may differ from a plain program's by a relative error of at most 0.022.
Values may be sent and summed in bfloat16 or wider, within the bound.
No kernel may reach another device: no remote copies, remote signals or barrier semaphores. Data moves between devices by JAX's collectives and lax.ppermute only.
A program may use at most 64 MiB of HBM per device.

v0:
```python
import jax
import jax.numpy as jnp
from jax import lax
from jax.sharding import PartitionSpec as P

epsilon = 1e-05


def layer_norm(values):
    average = jnp.mean(values, -1, keepdims=True)
    centred = values - average
    spread = jnp.mean(centred * centred, -1, keepdims=True)
    inverse = lax.rsqrt(spread + epsilon)
    return (centred * inverse, inverse)


def matmul(first, second):
    return jnp.dot(first, second, preferred_element_type=jnp.float32)


def on_device(pair, cotangent, w_gate_a, w_proj_a, w_gate_b, w_proj_b, w_gate_out, w_out):
    row_count, col_count, channels = pair.shape
    hidden = w_gate_a.shape[1]
    total_hidden = hidden * lax.axis_size("ch")
    out_width = cotangent.shape[2]
    length = row_count * lax.axis_size("row")
    grad_scale = 1.0 / length
    pair_hat, pair_rstd = layer_norm(pair.astype(jnp.float32))
    flat_norm = pair_hat.astype(jnp.bfloat16).reshape(row_count * col_count, channels)
    w_four = jnp.concatenate([w_gate_a, w_proj_a, w_gate_b, w_proj_b], axis=1)
    projected = matmul(flat_norm, w_four)
    gate_a = jax.nn.sigmoid(projected[:, :hidden])
    proj_a = projected[:, hidden : 2 * hidden]
    gate_b = jax.nn.sigmoid(projected[:, 2 * hidden : 3 * hidden])
    proj_b = projected[:, 3 * hidden :]
    left_edge = (gate_a * proj_a).astype(jnp.bfloat16).reshape(row_count, col_count, hidden)
    right_edge = (gate_b * proj_b).astype(jnp.bfloat16).reshape(row_count, col_count, hidden)
    right_all = lax.all_gather(right_edge, "row", axis=0, tiled=True)
    mixed_swap = lax.psum_scatter(
        jnp.einsum("jkh,ikh->jih", right_all, left_edge, preferred_element_type=jnp.float32).astype(
            jnp.bfloat16
        ),
        "col",
        scatter_dimension=0,
        tiled=True,
    ).astype(jnp.float32)
    mixed = jnp.swapaxes(mixed_swap, 0, 1).reshape(row_count * col_count, hidden)
    hidden_sums = lax.psum((jnp.sum(mixed, -1), jnp.sum(mixed * mixed, -1)), "ch")
    hidden_mean = (hidden_sums[0] / total_hidden)[:, None]
    hidden_var = (hidden_sums[1] / total_hidden)[:, None] - hidden_mean * hidden_mean
    hidden_rstd = lax.rsqrt(hidden_var + epsilon)
    mixed_hat = (mixed - hidden_mean) * hidden_rstd
    mixed_norm = mixed_hat.astype(jnp.bfloat16)
    norm_full = lax.all_gather(mixed_norm, "ch", axis=1, tiled=True)
    gate_out = jax.nn.sigmoid(matmul(flat_norm, w_gate_out))
    proj_out = matmul(norm_full, w_out)
    updated = (gate_out * proj_out).astype(jnp.bfloat16).reshape(row_count, col_count, out_width)
    upstream = cotangent.reshape(row_count * col_count, out_width).astype(jnp.float32)
    d_proj = (upstream * gate_out).astype(jnp.bfloat16)
    d_gate = (upstream * proj_out * gate_out * (1.0 - gate_out)).astype(jnp.bfloat16)
    head_grads = lax.psum(
        (matmul(norm_full.T, d_proj) * grad_scale, matmul(flat_norm.T, d_gate) * grad_scale),
        ("row", "col"),
    )
    d_norm = lax.psum_scatter(
        matmul(d_proj, w_out.T).astype(jnp.bfloat16), "ch", scatter_dimension=1, tiled=True
    ).astype(jnp.float32)
    back_sums = lax.psum((jnp.sum(d_norm, -1), jnp.sum(d_norm * mixed_hat, -1)), "ch")
    d_mixed = hidden_rstd * (
        d_norm
        - (back_sums[0] / total_hidden)[:, None]
        - mixed_hat * (back_sums[1] / total_hidden)[:, None]
    )
    d_mixed = d_mixed.astype(jnp.bfloat16).reshape(row_count, col_count, hidden)
    d_rows = lax.all_gather(d_mixed, "col", axis=1, tiled=True)
    right_back = lax.all_gather(right_edge, "row", axis=0, tiled=True)
    d_left = jnp.einsum("ijh,jkh->ikh", d_rows, right_back, preferred_element_type=jnp.float32)
    d_left = d_left.reshape(row_count * col_count, hidden)
    left_all = lax.all_gather(left_edge, "row", axis=0, tiled=True)
    d_columns = lax.all_to_all(d_rows, "row", split_axis=1, concat_axis=0, tiled=True)
    d_right = jnp.einsum("ijh,ikh->jkh", d_columns, left_all, preferred_element_type=jnp.float32)
    d_right = d_right.reshape(row_count * col_count, hidden)
    grad_pa = (d_left * gate_a).astype(jnp.bfloat16)
    grad_ga = (d_left * proj_a * gate_a * (1.0 - gate_a)).astype(jnp.bfloat16)
    grad_pb = (d_right * gate_b).astype(jnp.bfloat16)
    grad_gb = (d_right * proj_b * gate_b * (1.0 - gate_b)).astype(jnp.bfloat16)
    d_four = jnp.concatenate([grad_ga, grad_pa, grad_gb, grad_pb], axis=1)
    weight_terms = matmul(flat_norm.T, d_four) * grad_scale
    summed = lax.psum(weight_terms, ("row", "col"))
    d_flat = matmul(d_four, w_four.T) + matmul(d_gate, w_gate_out.T)
    hat_all = pair_hat.reshape(row_count * col_count, channels)
    rstd_flat = pair_rstd.reshape(row_count * col_count, 1)
    offset = lax.axis_index("ch") * out_width
    grad_whole = lax.psum(d_flat.astype(jnp.bfloat16), "ch").astype(jnp.float32)
    grad_full = rstd_flat * (
        grad_whole
        - jnp.mean(grad_whole, -1, keepdims=True)
        - hat_all * jnp.mean(grad_whole * hat_all, -1, keepdims=True)
    )
    grad_pair = lax.dynamic_slice_in_dim(grad_full, offset, out_width, 1)
    grad_pair = grad_pair.astype(jnp.bfloat16).reshape(row_count, col_count, out_width)
    return (
        updated,
        grad_pair,
        summed[:, :hidden],
        summed[:, hidden : 2 * hidden],
        summed[:, 2 * hidden : 3 * hidden],
        summed[:, 3 * hidden :],
        head_grads[1],
        head_grads[0],
    )


def solution(mesh):
    in_specs = (
        P("row", "col", None),
        P("row", "col", "ch"),
        P(None, "ch"),
        P(None, "ch"),
        P(None, "ch"),
        P(None, "ch"),
        P(None, "ch"),
        P(None, "ch"),
    )
    out_specs = (
        P("row", "col", "ch"),
        P("row", "col", "ch"),
        P(None, "ch"),
        P(None, "ch"),
        P(None, "ch"),
        P(None, "ch"),
        P(None, "ch"),
        P(None, "ch"),
    )
    return jax.shard_map(
        on_device, mesh=mesh, in_specs=in_specs, out_specs=out_specs, check_vma=False
    )
```

profile of v0, /device:TPU:0, one launch (start us, length us, event | category | flops | bytes accessed | tf_op | source)
XLA Modules:
  0.0 484.8 jit_solution(6996993139029059401)
XLA Ops:
  7.2 1.4 convert_reduce_fusion
  8.7 1.9 fusion.7
  10.6 0.8 fusion.4
  11.6 0.7 copy-done.4
  12.8 1.1 multiply_convert_fusion.7
  14.0 2.3 reshape.94
  16.4 2.3 reshape.93
  18.7 63.5 %all-gather.3.cloned.1.call-done = bf16[192,96,64]{1,0,2:T(8,128)(2,1)} async-done(((bf16[24,96,64]{1,0,2:T(8,128)(2,1)}), bf16[192,96,64]{1,0,2:T(8,128)(2,1)}) %all-gather.3.cloned.1.call-update) | async-done | bytes 2359312 | tf_op jit(solution)/shard_map/all_gather | solution.py:38
  82.2 4.7 fusion.6
  86.9 4.1 copy.60
  91.0 5.9 %reshape.103 = bf16[192,1536]{1,0:T(8,128)(2,1)} reshape(bf16[192,64,24]{2,1,0:T(8,128)(2,1)} %bitcast.63) | data formatting | bytes 1179648
  97.0 2.1 copy.47
  99.1 2.2 reshape.102
  101.3 9.3 %reduce-scatter.7.cloned.1.call-done = bf16[96,1536]{1,0:T(8,128)(2,1)} async-done(((bf16[192,1536]{1,0:T(8,128)(2,1)}), bf16[96,1536]{1,0:T(8,128)(2,1)}) %reduce-scatter.7.cloned.1.call-update) | async-done | bytes 294928
  110.5 4.3 reshape.104
  114.8 3.3 copy.61
  118.2 2.0 convert_bitcast_fusion
  120.2 0.8 fusion.22
  121.0 2.2 reshape.95
  123.1 1.4 reduce_sum.81
  124.5 1.4 reduce_sum.79
  125.9 4.6 all-reduce.2
  130.5 0.7 broadcast_multiply_fusion.4
  131.3 1.1 fusion.21
  132.4 2.4 all_gather.14
  134.8 0.8 copy-done.1
  135.9 1.3 multiply_convert_fusion
  137.9 1.2 convolution_convert_fusion
  139.7 7.6 %reduce-scatter.5.cloned.1.call-done = bf16[2304,64]{0,1:T(8,128)(2,1)} async-done(((bf16[2304,128]{0,1:T(8,128)(2,1)}), bf16[2304,64]{0,1:T(8,128)(2,1)}) %reduce-scatter.5.cloned.1.call-update) | async-done | bytes 294928 | tf_op jit(solution)/shard_map/reduce_scatter | solution.py:65
  147.3 1.9 convert_reduce_fusion.1
  149.2 4.6 all-reduce.1
  153.8 0.7 broadcast_multiply_fusion.2
  154.5 2.0 fusion.13
  156.6 2.3 reshape.97
  158.9 2.3 copy.48
  161.2 21.8 %all_gather.15 = bf16[24,192,64]{2,0,1:T(8,128)(2,1)} all-gather(bf16[24,96,64]{2,0,1:T(8,128)(2,1)} %copy.48), channel_id=1, replica_groups=mesh['row'=8,'col'=2,'ch'=2] {'col'}, dimensions={1}, use_global_device_ids=true | all-gather | bytes 884736 | tf_op jit(solution)/shard_map/all_gather | solution.py:75
  183.0 3.2 reshape.105
  186.2 5.5 %all-to-all-start = ((bf16[8,2,18432]{2,1,0:T(2,128)(2,1)}), bf16[8,2,18432]{2,1,0:T(2,128)(2,1)}, u32[]{:S(2)}, u32[]{:S(2)}) async-start(bf16[8,2,18432]{2,1,0:T(2,128)(2,1)} %reshape.105), calls=%async_computation.1 | async-start | bytes 1179648 | tf_op jit(solution)/shard_map/all_to_all | solution.py:80
  191.8 3.1 copy.49
  194.8 4.0 convolution_bitcast_fusion.1
  198.8 2.2 reshape.98
  200.9 21.1 %all-to-all-done = bf16[8,2,18432]{2,1,0:T(2,128)(2,1)} async-done(((bf16[8,2,18432]{2,1,0:T(2,128)(2,1)}), bf16[8,2,18432]{2,1,0:T(2,128)(2,1)}, u32[]{:S(2)}, u32[]{:S(2)}) %all-to-all-start) | async-done | bytes 589856 | tf_op jit(solution)/shard_map/all_to_all | solution.py:80
  222.1 3.2 reshape.106
  225.3 2.5 copy.51
  227.8 3.0 copy.52
  230.8 3.9 convolution_bitcast_fusion
  234.7 2.2 reshape.99
  237.0 1.7 multiply_convert_fusion.4
  238.7 1.6 fusion.23
  240.3 1.2 convolution_multiply_fusion
  241.6 2.5 fusion
  244.4 1.7 reshape.96
  246.1 0.8 copy.53
  246.9 0.8 convolution_multiply_fusion.1
  247.8 0.9 convolution_multiply_fusion.2
  248.7 95.6 %all-reduce.9.cloned.1.call-done = f32[128,256]{1,0:T(8,128)} async-done(((f32[128,256]{1,0:T(8,128)}), f32[128,256]{1,0:T(8,128)}) %all-reduce.9.cloned.1.call-update) | async-done | bytes 131088 | tf_op jit(solution)/shard_map/psum | solution.py:89
  344.3 1.0 fusion.27
  348.2 16.3 %all-reduce.7.cloned.1.call-done = bf16[2304,128]{1,0:T(8,128)(2,1)} async-done(((bf16[2304,128]{1,0:T(8,128)(2,1)}), bf16[2304,128]{1,0:T(8,128)(2,1)}) %all-reduce.7.cloned.1.call-update) | async-done | bytes 589840 | tf_op jit(solution)/shard_map/psum | solution.py:94
  364.5 1.7 convert_reduce_fusion.2
  366.3 1.7 fusion.10
  368.0 1.0 copy.54
  369.0 106.2 %all-reduce.11.cloned.1.call-done = (f32[128,64]{0,1:T(8,128)}, f32[128,64]{0,1:T(8,128)}) async-done(((f32[128,64]{0,1:T(8,128)}, f32[128,64]{0,1:T(8,128)}), (f32[128,64]{0,1:T(8,128)}, f32[128,64]{0,1:T(8,128)})) %all-reduce.11.cloned.1.call-update) | async-done | bytes 65552 | tf_op jit(solution)/shard_map/psum | solution.py:61
  475.2 1.4 copy.69
  476.6 1.4 copy.70
  (77 shorter events, 5.7 us)
Async XLA Ops:
  7.2 128.7 %copy-start = (bf16[128,64]{0,1:T(8,128)(2,1)S(1)}, bf16[128,64]{0,1:T(8,128)(2,1)}, u32[]{:S(2)}) copy-start(bf16[128,64]{0,1:T(8,128)(2,1)} %param.14) | copy-start | bytes 49156
  7.2 3.4 copy-start.3
  7.2 75.0 %all-gather.3.cloned.1.call-start = ((), (), s32[]{:S(2)}) async-start(), calls=%async_computation.3 | async-start | bytes 3538944 | tf_op jit(solution)/shard_map/all_gather | solution.py:38
  10.6 0.9 copy-start.15
  10.6 0.9 copy-start.20
  10.6 0.9 copy-start.21
  10.6 0.9 copy-start.22
  10.6 0.9 copy-start.23
  11.5 0.8 copy-start.4
  11.6 0.8 copy-start.17
  16.3 94.2 %reduce-scatter.7.cloned.1.call-start = ((), (), s32[]{:S(2)}) async-start(), calls=%async_computation.8 | async-start | bytes 884736
  96.9 50.4 %reduce-scatter.5.cloned.1.call-start = ((), (), s32[]{:S(2)}) async-start(), calls=%async_computation.4 | async-start | bytes 884736 | tf_op jit(solution)/shard_map/reduce_scatter | solution.py:65
  118.2 2.0 copy-start.7
  130.5 5.1 %copy-start.19 = (bf16[128,64]{0,1:T(8,128)(2,1)S(1)}, bf16[128,64]{0,1:T(8,128)(2,1)}, u32[]{:S(2)}) copy-start(bf16[128,64]{0,1:T(8,128)(2,1)} %param.15) | copy-start | bytes 49156
  131.3 3.5 copy-start.13
  131.3 3.5 copy-start.14
  132.4 3.5 copy-start.5
  132.4 3.5 copy-start.12
  134.8 0.8 copy-start.1
  137.2 0.7 copy-start.9
  139.1 91.7 %all-gather.5.cloned.1.call-start = ((), (), s32[]{:S(2)}) async-start(), calls=%async_computation.5 | async-start | bytes 3538944 | tf_op jit(solution)/shard_map/all_gather | solution.py:79
  186.2 35.9 %all-to-all-start = ((bf16[8,2,18432]{2,1,0:T(2,128)(2,1)}), bf16[8,2,18432]{2,1,0:T(2,128)(2,1)}, u32[]{:S(2)}, u32[]{:S(2)}) async-start(bf16[8,2,18432]{2,1,0:T(2,128)(2,1)} %reshape.105), calls=%async_computation.1 | async-start | bytes 1179648 | tf_op jit(solution)/shard_map/all_to_all | solution.py:80
  191.7 152.6 %all-reduce.9.cloned.1.call-start = ((), (), s32[]{:S(2)}) async-start(), calls=%async_computation.7 | async-start | bytes 262144 | tf_op jit(solution)/shard_map/psum | solution.py:89
  237.0 1.7 copy-start.18
  238.7 1.6 copy-start.6
  240.3 1.3 copy-start.11
  241.5 123.0 %all-reduce.7.cloned.1.call-start = ((), (), s32[]{:S(2)}) async-start(), calls=%async_computation.6 | async-start | bytes 1179648 | tf_op jit(solution)/shard_map/psum | solution.py:94
  241.6 2.8 copy-start.16
  244.1 231.1 %all-reduce.11.cloned.1.call-start = ((), (), s32[]{:S(2)}) async-start(), calls=%async_computation.9 | async-start | bytes 131072 | tf_op jit(solution)/shard_map/psum | solution.py:61
  244.4 3.4 copy-start.2
  244.4 3.4 copy-start.10
  364.5 1.7 copy-start.8
Sparse Core Ops, SparseCore 0:
  16.4 65.7 all-gather.2
  97.0 13.4 reduce-scatter.6
  139.2 8.0 reduce-scatter.4
  149.8 74.7 all-gather.4
  241.6 102.6 all-reduce.8
  346.6 17.8 all-reduce.6
  371.6 103.5 all-reduce.10
where the time goes:
time: 487 us; the launch traced here: 485 us
  waiting for transfers between devices  320 us (66%)
  local copies, waits for them, and re-layouts  68.1 us (14%)
  blocking collectives  33.4 us (7%)
  matrix products  22.7 us (5%)
  other arithmetic  19.8 us (4%)
  between operations  14.5 us (3%)
  starting transfers between devices  6.19 us (1%)
    psum x1, waiting for transfers between devices, on_device(): lax.psum((matmul(norm_full.T, d_proj) * grad_scale, matmul(flat_norm.T, d...  106 us
    psum x1, waiting for transfers between devices, on_device(): summed = lax.psum(weight_terms, ('row', 'col'))  95.6 us
    all_gather x1, waiting for transfers between devices, on_device(): right_all = lax.all_gather(right_edge, 'row', axis=0, tiled=True)  63.5 us
    unnamed x65, local copies, waits for them, and re-layouts  33.9 us
    all_gather x1, blocking collectives, on_device(): d_rows = lax.all_gather(d_mixed, 'col', axis=1, tiled=True)  21.8 us
    all_to_all x1, waiting for transfers between devices, on_device(): lax.all_to_all(d_rows, 'row', split_axis=1, concat_axis=0, tiled=True)  21.1 us
    psum x1, waiting for transfers between devices, on_device(): grad_whole = lax.psum(d_flat.astype(jnp.bfloat16), 'ch').astype(jnp.float32)  16.3 us
    dot_general x9, matrix products, matmul(): return jnp.dot(first, second, preferred_element_type=jnp.float32)  10.2 us
  transfers between devices with their start and end apart: 8, of which 7 were waited for; matrix products, arithmetic and copies ran while one was open for 11% of the time, Pallas kernels for 0%

commit v1 on v0

--- a/solution.py
+++ b/solution.py
@@ -1,6 +1,11 @@
+import functools
+
 import jax
 import jax.numpy as jnp
+import numpy as np
 from jax import lax
+from jax.experimental import pallas as pl
+from jax.experimental.pallas import tpu as pltpu
 from jax.sharding import PartitionSpec as P
 
 epsilon = 1e-05
@@ -18,7 +23,7 @@
     return jnp.dot(first, second, preferred_element_type=jnp.float32)
 
 
-def on_device(pair, cotangent, w_gate_a, w_proj_a, w_gate_b, w_proj_b, w_gate_out, w_out):
+def by_rows(pair, cotangent, w_gate_a, w_proj_a, w_gate_b, w_proj_b, w_gate_out, w_out):
     row_count, col_count, channels = pair.shape
     hidden = w_gate_a.shape[1]
     total_hidden = hidden * lax.axis_size("ch")
@@ -111,6 +116,343 @@
     )
 
 
+everyone = ("col", "row", "ch")
+f32, bf16 = jnp.float32, jnp.bfloat16
+
+
+def dot(first, second, over):
+    return lax.dot_general(
+        first, second, (((over[0],), (over[1],)), ((), ())), preferred_element_type=f32
+    )
+
+
+def call(kernel, outs, args, scratch=()):
+    whole = pl.BlockSpec(memory_space=pltpu.VMEM)
+    scalars = pl.BlockSpec(memory_space=pltpu.SMEM)
+    return pl.pallas_call(
+        kernel,
+        out_shape=tuple(jax.ShapeDtypeStruct(*out) for out in outs),
+        in_specs=[scalars if arg.dtype == jnp.int32 else whole for arg in args],
+        out_specs=tuple(whole for _ in outs),
+        scratch_shapes=scratch,
+        compiler_params=pltpu.CompilerParams(vmem_limit_bytes=50 * 2**20),
+    )(*args)
+
+
+def grouping(hidden, share):
+    rows = np.arange(2 * hidden)
+    group, side, rest = rows // (2 * share), (rows // share) % 2, rows % share
+    return (np.arange(2 * hidden)[None] == (side * hidden + group * share + rest)[:, None])
+
+
+def turn_weights(order, ga, pa, gb, pb, go, wo, out):
+    width = order.shape[0]
+    order = order[...]
+    out[:width] = dot(order, jnp.concatenate([ga[...], gb[...]], axis=1), (1, 1)).astype(bf16)
+    out[width : 2 * width] = dot(
+        order, jnp.concatenate([pa[...], pb[...]], axis=1), (1, 1)
+    ).astype(bf16)
+    last = jnp.concatenate([go[...], wo[...]], axis=1).astype(f32).T
+    out[2 * width :] = last.astype(bf16)
+
+
+def rows_of(weights, start, count):
+    return jnp.concatenate([weights[c, start : start + count] for c in range(weights.shape[0])], 0)
+
+
+def edges(width, half, pair, weights, send, normed, hat, inverse):
+    count, cols, channels = pair.shape
+    count = count // weights.shape[0]
+    values = pair[pl.ds(half[0] * count, count)].astype(f32).reshape(count * cols, channels).T
+    centred = values - jnp.mean(values, 0, keepdims=True)
+    rstd = lax.rsqrt(jnp.mean(centred * centred, 0, keepdims=True) + epsilon)
+    hat[...] = centred * rstd
+    inverse[...] = rstd
+    normed[...] = (centred * rstd).astype(bf16)
+    gate = jax.nn.sigmoid(dot(rows_of(weights, 0, width), normed[...], (1, 0)))
+    value = dot(rows_of(weights, width, width), normed[...], (1, 0))
+    send[...] = (gate * value).reshape(send.shape).astype(bf16)
+
+
+def gates(width, half, normed, weights, own, other, gate_out, upstream):
+    parts, total, _ = weights.shape
+    hidden = (total - 2 * width) // 2
+    count, cols, _ = other.shape
+    gate_out[...] = jax.nn.sigmoid(dot(rows_of(weights, 2 * width, hidden), normed[...], (1, 0)))
+    mine = own[pl.ds(half[0] * count, count)].astype(f32).reshape(count * cols, hidden).T
+    yours = other[...].astype(f32).reshape(count * cols, hidden).T
+    upstream[pl.ds(pl.multiple_of(half[0] * hidden, hidden), hidden)] = mine
+    upstream[pl.ds(pl.multiple_of((1 - half[0]) * hidden, hidden), hidden)] = yours
+
+
+def spread_rows(block, cols, arrived, held):
+    devices, q, flat = arrived.shape
+
+    def one(s, _):
+        tile = arrived[s].astype(f32)
+        for i in range(flat // cols):
+            start = pl.multiple_of((s * (flat // cols) + i) * block, block)
+            held[pl.ds(start, q), 0:cols] = tile[:, i * cols : (i + 1) * cols]
+        return 0
+
+    lax.fori_loop(0, devices, one, 0)
+
+
+def pack_rows(block, cols, held, send):
+    devices, q, flat = send.shape
+
+    def one(s, _):
+        pieces = []
+        for i in range(flat // cols):
+            start = pl.multiple_of((s * (flat // cols) + i) * block, block)
+            pieces.append(held[pl.ds(start, block), 0:cols])
+        send[s] = jnp.concatenate(pieces, axis=1)[:q].astype(bf16)
+        return 0
+
+    lax.fori_loop(0, devices, one, 0)
+
+
+def mix(parts, cols, arrived, send, kept, held, result):
+    block = 8
+    q = arrived.shape[1]
+    tokens = held.shape[0] // (parts * block)
+    spread_rows(block, cols, arrived, held)
+    for p in range(parts):
+        for e in range(q):
+            start = p * tokens * block + e
+            kept[e, p] = held[pl.ds(start, tokens, stride=block), 0:cols].astype(bf16)
+    for e in range(q // 2):
+        for p in range(parts):
+            total = 0.0
+            for k in range(parts):
+                total = total + dot(
+                    kept[e, k], kept[q // 2 + e, k, p * cols : (p + 1) * cols], (1, 1)
+                )
+            result[pl.ds(p * tokens * block + e, tokens, stride=block), 0:cols] = total
+    pack_rows(block, cols, result, send)
+
+
+def head(width, arrived, weights, gate_out, upstream, send, hat_rounded, d_proj, d_gate, updated):
+    parts, total, _ = weights.shape
+    hidden = (total - 2 * width) // 2
+    devices, q, flat = arrived.shape
+    mixed = jnp.concatenate([arrived[s].astype(f32) for s in range(devices)], 0)
+    average = jnp.mean(mixed, 0, keepdims=True)
+    spread = jnp.mean(mixed * mixed, 0, keepdims=True) - average * average
+    inverse = lax.rsqrt(spread + epsilon)
+    hat = (mixed - average) * inverse
+    hat_rounded[...] = hat.astype(bf16)
+    w_out = rows_of(weights, 2 * width + hidden, hidden)
+    proj = dot(w_out, hat_rounded[...], (1, 0))
+    gate = gate_out[...]
+    up = upstream[...]
+    d_proj[...] = (up * gate).astype(bf16)
+    d_gate[...] = (up * proj * gate * (1.0 - gate)).astype(bf16)
+    updated[...] = (gate * proj).astype(bf16)
+    d_norm = dot(w_out, d_proj[...], (0, 0))
+    d_mixed = inverse * (
+        d_norm
+        - jnp.mean(d_norm, 0, keepdims=True)
+        - hat * jnp.mean(d_norm * hat, 0, keepdims=True)
+    )
+    for s in range(devices):
+        send[s] = d_mixed[s * q : (s + 1) * q].astype(bf16)
+
+
+def head_rest(parts, scale, normed, hat_rounded, d_proj, d_gate, updated, terms, updated_rows):
+    hidden = d_gate.shape[0] // parts
+    by_gate = dot(d_gate[...], normed[...], (1, 1)) * scale
+    by_out = dot(d_proj[...], hat_rounded[...], (1, 1)) * scale
+    for c in range(parts):
+        terms[c, :hidden] = by_gate[c * hidden : (c + 1) * hidden]
+        terms[c, hidden:] = by_out[c * hidden : (c + 1) * hidden]
+    turned = updated[...].astype(f32).T
+    for c in range(parts):
+        updated_rows[c] = turned[:, c * hidden : (c + 1) * hidden].reshape(
+            updated_rows.shape[1:]
+        ).astype(bf16)
+
+
+def unmix(parts, cols, arrived, kept, send, held, result):
+    block = 8
+    q = arrived.shape[1]
+    tokens = held.shape[0] // (parts * block)
+    spread_rows(block, cols, arrived, held)
+    for e in range(q):
+        d_mixed = [
+            held[pl.ds(p * tokens * block + e, tokens, stride=block), 0:cols].astype(bf16)
+            for p in range(parts)
+        ]
+        for k in range(parts):
+            total = 0.0
+            for p in range(parts):
+                total = total + dot(
+                    d_mixed[p], kept[q + e, k, p * cols : (p + 1) * cols], (1, 0)
+                )
+                start = (k * tokens + p * cols) * block + q + e
+                result[pl.ds(start, cols, stride=block), 0:cols] = dot(
+                    d_mixed[p], kept[e, k], (0, 0)
+                )
+            result[pl.ds(k * tokens * block + e, tokens, stride=block), 0:cols] = total
+    pack_rows(block, cols, result, send)
+
+
+def tail(width, scale, arrived, weights, normed, hat, inverse, d_gate, head_terms, send, grad_rows):
+    parts, total, channels = weights.shape
+    hidden = (total - 2 * width) // 2
+    devices, q, flat = arrived.shape
+    w_gate, w_value = rows_of(weights, 0, width), rows_of(weights, width, width)
+    gate = jax.nn.sigmoid(dot(w_gate, normed[...], (1, 0)))
+    value = dot(w_value, normed[...], (1, 0))
+    grad = arrived[...].astype(f32).reshape(devices * q, flat)
+    by_value = grad * gate
+    by_gate = (by_value * (value * (1.0 - gate))).astype(bf16)
+    by_value = by_value.astype(bf16)
+    terms = [
+        dot(by_gate, normed[...], (1, 1)) * scale,
+        dot(by_value, normed[...], (1, 1)) * scale,
+    ]
+    per = send.shape[1]
+    for c in range(parts):
+        whole = jnp.concatenate(
+            [term[c * width : (c + 1) * width] for term in terms] + [head_terms[c]], 0
+        )
+        for s in range(total // per):
+            send[c * (total // per) + s] = whole[s * per : (s + 1) * per].astype(bf16)
+    d_input = dot(w_gate, by_gate, (0, 0)) + dot(w_value, by_value, (0, 0))
+    d_input = d_input + dot(rows_of(weights, 2 * width, hidden), d_gate[...], (0, 0))
+    back = inverse[...] * (
+        d_input
+        - jnp.mean(d_input, 0, keepdims=True)
+        - hat[...] * jnp.mean(d_input * hat[...], 0, keepdims=True)
+    )
+    turned = back.T
+    for c in range(parts):
+        grad_rows[c] = turned[:, c * hidden : (c + 1) * hidden].reshape(
+            grad_rows.shape[1:]
+        ).astype(bf16)
+
+
+def add_up(arrived, out):
+    out[...] = jnp.sum(arrived[...].astype(f32), 0).astype(bf16)
+
+
+def turn_back(order, sums, ga, pa, gb, pb, go, wo):
+    width = order.shape[0]
+    hidden = width // 2
+    order = order[...]
+    whole = jnp.concatenate([sums[s].astype(f32) for s in range(sums.shape[0])], 0)
+    for at, (left, right) in enumerate(((ga, gb), (pa, pb))):
+        both = dot(whole[at * width : (at + 1) * width].astype(bf16), order, (0, 0))
+        left[...] = both[:, :hidden]
+        right[...] = both[:, hidden:]
+    both = whole[2 * width :].T
+    go[...] = both[:, :hidden]
+    wo[...] = both[:, hidden:]
+
+
+def by_channels(pair, cotangent, w_gate_a, w_proj_a, w_gate_b, w_proj_b, w_gate_out, w_out):
+    row_count, cols, channels = pair.shape
+    hidden = w_gate_a.shape[1]
+    parts = lax.axis_size("ch")
+    col_parts = lax.axis_size("col")
+    devices = lax.axis_size(everyone)
+    share = hidden * parts // devices
+    width = 2 * hidden
+    count = row_count // parts
+    flat = count * cols
+    tokens = cols * col_parts
+    scale = 1.0 / tokens
+    half = lax.axis_index("ch").astype(jnp.int32).reshape(1)
+    order = jnp.asarray(grouping(hidden, share), bf16)
+    swap = [(c, parts - 1 - c) for c in range(parts)]
+
+    (weights,) = call(
+        turn_weights,
+        [((2 * width + 2 * hidden, channels), bf16)],
+        (order, w_gate_a, w_proj_a, w_gate_b, w_proj_b, w_gate_out, w_out),
+    )
+    weights = lax.all_gather(weights, "ch")
+    other = lax.dynamic_slice_in_dim(cotangent, (1 - half[0]) * count, count, 0)
+    other = lax.ppermute(other, "ch", swap)
+    send, normed, hat, inverse = call(
+        functools.partial(edges, width),
+        [
+            ((devices, 2 * share, flat), bf16),
+            ((channels, flat), bf16),
+            ((channels, flat), f32),
+            ((1, flat), f32),
+        ],
+        (half, pair, weights),
+    )
+    arrived = lax.all_to_all(send, everyone, 0, 0)
+    gate_out, upstream = call(
+        functools.partial(gates, width),
+        [((hidden * parts, flat), f32)] * 2,
+        (half, normed, weights, cotangent, other),
+    )
+    room = pltpu.VMEM((col_parts * tokens * 8, -(-cols // 128) * 128), f32)
+    send, kept = call(
+        functools.partial(mix, col_parts, cols),
+        [((devices, share, flat), bf16), ((2 * share, col_parts, tokens, cols), bf16)],
+        (arrived,),
+        (room, room),
+    )
+    arrived = lax.all_to_all(send, everyone, 0, 0)
+    send, hat_rounded, d_proj, d_gate, updated = call(
+        functools.partial(head, width),
+        [((devices, share, flat), bf16)] + [((hidden * parts, flat), bf16)] * 4,
+        (arrived, weights, gate_out, upstream),
+    )
+    arrived = lax.all_to_all(send, everyone, 0, 0)
+    head_terms, updated_rows = call(
+        functools.partial(head_rest, parts, scale),
+        [((parts, 2 * hidden, channels), f32), ((parts, count, cols, hidden), bf16)],
+        (normed, hat_rounded, d_proj, d_gate, updated),
+    )
+    updated = lax.all_to_all(updated_rows, "ch", 0, 0).reshape(row_count, cols, hidden)
+    (send,) = call(
+        functools.partial(unmix, col_parts, cols),
+        [((devices, 2 * share, flat), bf16)],
+        (arrived, kept),
+        (room, room),
+    )
+    arrived = lax.all_to_all(send, everyone, 0, 0)
+    per = (2 * width + 2 * hidden) * parts // devices
+    send, grad_rows = call(
+        functools.partial(tail, width, scale),
+        [((devices, per, channels), bf16), ((parts, count, cols, hidden), bf16)],
+        (arrived, weights, normed, hat, inverse, d_gate, head_terms),
+    )
+    arrived = lax.all_to_all(send, ("ch", "row", "col"), 0, 0)
+    grad_pair = lax.all_to_all(grad_rows, "ch", 0, 0).reshape(row_count, cols, hidden)
+    (sums,) = call(add_up, [((per, channels), bf16)], (arrived,))
+    rest = devices // parts
+    sums = lax.all_to_all(
+        jnp.broadcast_to(sums[None], (rest, per, channels)), ("row", "col"), 0, 0
+    )
+    ga, pa, gb, pb, go, wo = call(
+        turn_back, [((channels, hidden), f32)] * 6, (order, sums)
+    )
+    return updated, grad_pair, ga, pa, gb, pb, go, wo
+
+
+def on_device(*arrays):
+    row_count, cols, _ = arrays[0].shape
+    parts, devices = lax.axis_size("ch"), lax.axis_size(everyone)
+    hidden = arrays[2].shape[1]
+    share = hidden * parts // devices
+    fits = (
+        share * devices == hidden * parts
+        and parts == 2
+        and 2 * share == 8
+        and row_count % parts == 0
+        and arrays[1].shape[2] == hidden
+        and cols % 16 == 0
+    )
+    return by_channels(*arrays) if fits else by_rows(*arrays)
+
+
 def solution(mesh):
     in_specs = (
         P("row", "col", None),

time: 487 us -> 141 us (0.29)
  waiting for transfers between devices: 320 us -> 42.2 us
  local copies, waits for them, and re-layouts: 68.1 us -> 20 us
  matrix products: 22.7 us -> 0 us
  other arithmetic: 19.8 us -> 0 us
  Pallas kernels: 0 us -> 17.7 us
  between operations: 14.5 us -> 0.84 us
  blocking collectives: 33.4 us -> 43.6 us
  starting transfers between devices: 6.19 us -> 15.2 us
    psum x3 -> x0, waiting for transfers between devices: 218 us -> none  [the longest x1 106 us: on_device(): lax.psum((matmul(norm_full.T, d_proj) * grad_scale, matmul(flat_norm.T, d...]
    all_gather x2 -> x0, waiting for transfers between devices: 63.5 us -> none  [the longest x1 63.5 us: on_device(): right_all = lax.all_gather(right_edge, 'row', axis=0, tiled=True)]
    all_to_all x0 -> x3, blocking collectives: none -> 41.6 us  [the longest x2 37.5 us: by_channels(): arrived = lax.all_to_all(send, everyone, 0, 0)]
    dot_general x12 -> x0, matrix products: 22.7 us -> none  [the longest x9 10.2 us: matmul(): return jnp.dot(first, second, preferred_element_type=jnp.float32)]
    all_gather x2 -> x1, blocking collectives: 24.2 us -> 2.04 us  [by_channels(): weights = lax.all_gather(weights, 'ch')]
    all_to_all x1 -> x5, waiting for transfers between devices: 21.1 us -> 40.8 us  [the longest x2 23.1 us: by_channels(): arrived = lax.all_to_all(send, everyone, 0, 0)]
    pallas_call x0 -> x10, Pallas kernels: none -> 17.7 us  [call(): pl.pallas_call(kernel, out_shape=tuple((jax.ShapeDtypeStruct(*out) for ou...]
    reshape x8 -> x0, local copies, waits for them, and re-layouts: 17.5 us -> none  [the longest x2 4.59 us: on_device(): d_mixed = d_mixed.astype(jnp.bfloat16).reshape(row_count, col_count, hidden)]
  transfers between devices with their start and end apart: 8 -> 6, of which waited for: 7 -> 6; matrix products, arithmetic and copies ran while one was open for 11% -> 1% of each run, Pallas kernels for 0% -> 0%
where the time goes in v1:
time: 141 us; the launch traced here: 140 us
  blocking collectives  43.6 us (31%)
  waiting for transfers between devices  42.2 us (30%)
  local copies, waits for them, and re-layouts  20 us (14%)
  Pallas kernels  17.7 us (13%)
  starting transfers between devices  15.2 us (11%)
    all_to_all x2, blocking collectives, by_channels(): arrived = lax.all_to_all(send, everyone, 0, 0)  37.5 us
    all_to_all x2, waiting for transfers between devices, by_channels(): arrived = lax.all_to_all(send, everyone, 0, 0)  23.1 us
    unnamed x41, local copies, waits for them, and re-layouts  18.1 us
    pallas_call x10, Pallas kernels, call(): pl.pallas_call(kernel, out_shape=tuple((jax.ShapeDtypeStruct(*out) for ou...  17.7 us
    all_to_all x1, waiting for transfers between devices, by_channels(): arrived = lax.all_to_all(send, ('ch', 'row', 'col'), 0, 0)  8.47 us
    all_to_all x1, waiting for transfers between devices, by_channels(): lax.all_to_all(jnp.broadcast_to(sums[None], (rest, per, channels)), ('row...  7.63 us
    all_to_all x2, starting transfers between devices, by_channels(): arrived = lax.all_to_all(send, everyone, 0, 0)  5.46 us
    all_to_all x1, blocking collectives, by_channels(): lax.all_to_all(grad_rows, 'ch', 0, 0).reshape(row_count, cols, hidden)  4.04 us
  transfers between devices with their start and end apart: 6, of which 6 were waited for; matrix products, arithmetic and copies ran while one was open for 1% of the time, Pallas kernels for 0%

profile of v1, /device:TPU:0, one launch (start us, length us, event | category | flops | bytes accessed | tf_op | source)
XLA Modules:
  0.0 139.6 jit_solution(6020740778279790211)
XLA Ops:
  0.6 0.0 copy-start.11
  0.6 0.0 copy-start.4
  0.7 0.9 copy.33.ga
  1.5 0.8 copy.34.pa
  2.4 0.8 copy.35.gb
  3.2 0.8 copy.36.pb
  4.1 0.8 copy.37.go
  4.9 0.8 copy.38.wo
  5.7 0.0 copy-done.11
  5.7 0.2 shard_map.152
  6.0 2.0 %all-gather = bf16[768,128]{1,0:T(8,128)(2,1)S(1)} all-gather(bf16[384,128]{1,0:T(8,128)(2,1)S(1)} %shard_map.152), channel_id=2, replica_groups=mesh['row'=8,'col'=2,'ch'=2] {'ch'}, dimensions={0}, use_global_device_ids=true | all-gather | bytes 294912 | tf_op jit(solution)/shard_map/all_gather | solution.py:375
  8.0 0.0 copy-done.4
  8.0 0.7 shard_map.153
  8.7 24.3 %all_to_all.40.arrived = bf16[32,8,1152]{2,1,0:T(8,128)(2,1)S(1)} all-to-all(bf16[32,8,1152]{2,1,0:T(8,128)(2,1)S(1)} %get-tuple-element.32), channel_id=1, replica_groups=mesh['row'=8,'col'=2,'ch'=2] {'col','row','ch'}, dimensions={0} | all-to-all | bytes 1179648 | tf_op jit(solution)/shard_map/all_to_all | solution.py:388
  33.1 6.5 %shard_map.154 = (bf16[32,4,1152]{2,1,0:T(4,128)(2,1)}, bf16[8,2,192,96]{3,2,1,0:T(8,128)(2,1)S(1)}) custom-call(bf16[32,8,1152]{2,1,0:T(8,128)(2,1)S(1)} %all_to_all.40.arrived), custom_call_target="tpu_custom_call" | custom-call | tf_op jit(solution)/shard_map/pallas_call | solution.py:132
  39.5 0.0 copy-start.12
  39.5 2.7 %all-to-all-start.1 = ((bf16[32,4,1152]{2,1,0:T(4,128)(2,1)}), bf16[32,4,1152]{2,1,0:T(4,128)(2,1)S(1)}, u32[]{:S(2)}, u32[]{:S(2)}) async-start(bf16[32,4,1152]{2,1,0:T(4,128)(2,1)} %get-tuple-element.33), calls=%async_computation.1 | async-start | bytes 589824 | tf_op jit(solution)/shard_map/all_to_all | solution.py:401
  42.3 0.0 copy-done.12
  42.3 0.3 copy.40.own
  42.6 0.2 collective-permute-start
  42.8 1.5 %collective-permute-done.other = bf16[12,96,64]{2,1,0:T(8,128)(2,1)S(1)} collective-permute-done((bf16[12,96,64]{2,1,0:T(8,128)(2,1)S(1)}, bf16[12,96,64]{2,1,0:T(8,128)(2,1)S(1)}, u32[]{:S(2)}, u32[]{:S(2)}) %collective-permute-start) | collective-permute-done | bytes 147488 | tf_op jit(solution)/shard_map/ppermute | solution.py:377
  44.3 0.3 shard_map.155
  44.5 0.0 copy-start
  44.6 0.8 copy-done
  45.4 0.0 copy-start.2
  45.4 0.8 copy-done.2
  46.2 7.1 %all-to-all-done.1.arrived = bf16[32,4,1152]{2,1,0:T(4,128)(2,1)S(1)} async-done(((bf16[32,4,1152]{2,1,0:T(4,128)(2,1)}), bf16[32,4,1152]{2,1,0:T(4,128)(2,1)S(1)}, u32[]{:S(2)}, u32[]{:S(2)}) %all-to-all-start.1) | async-done | bytes 294944 | tf_op jit(solution)/shard_map/all_to_all | solution.py:401
  53.3 1.1 copy-done.1
  54.3 1.1 copy-done.3
  55.4 0.7 shard_map.156
  56.1 0.0 copy-start.7
  56.1 0.7 copy-done.7
  56.8 0.7 copy-done.9
  57.5 13.2 %all_to_all.41.arrived = bf16[32,4,1152]{2,1,0:T(4,128)(2,1)S(1)} all-to-all(bf16[32,4,1152]{2,1,0:T(4,128)(2,1)S(1)} %get-tuple-element.41), channel_id=1, replica_groups=mesh['row'=8,'col'=2,'ch'=2] {'col','row','ch'}, dimensions={0} | all-to-all | bytes 589824 | tf_op jit(solution)/shard_map/all_to_all | solution.py:407
  70.7 6.4 %shard_map.158 = bf16[32,8,1152]{2,1,0:T(8,128)(2,1)} custom-call(bf16[32,4,1152]{2,1,0:T(4,128)(2,1)S(1)} %all_to_all.41.arrived, bf16[8,2,192,96]{3,2,1,0:T(8,128)(2,1)S(1)} %get-tuple-element.42.kept), custom_call_target="tpu_custom_call" | custom-call | tf_op jit(solution)/shard_map/pallas_call | solution.py:132
  77.1 2.7 %all-to-all-start.4 = ((bf16[32,8,1152]{2,1,0:T(8,128)(2,1)}), bf16[32,8,1152]{2,1,0:T(8,128)(2,1)S(1)}, u32[]{:S(2)}, u32[]{:S(2)}) async-start(bf16[32,8,1152]{2,1,0:T(8,128)(2,1)} %shard_map.158), calls=%async_computation.4 | async-start | bytes 1179648 | tf_op jit(solution)/shard_map/all_to_all | solution.py:420
  79.9 0.0 copy-done.8
  79.9 0.0 copy-start.10
  79.9 1.0 copy-done.10
  80.9 0.4 shard_map.157
  81.2 16.0 %all-to-all-done.4.arrived = bf16[32,8,1152]{2,1,0:T(8,128)(2,1)S(1)} async-done(((bf16[32,8,1152]{2,1,0:T(8,128)(2,1)}), bf16[32,8,1152]{2,1,0:T(8,128)(2,1)S(1)}, u32[]{:S(2)}, u32[]{:S(2)}) %all-to-all-start.4) | async-done | bytes 589856 | tf_op jit(solution)/shard_map/all_to_all | solution.py:420
  97.2 2.2 %shard_map.159 = (bf16[32,24,128]{2,1,0:T(8,128)(2,1)}, bf16[2,12,96,64]{3,2,1,0:T(8,128)(2,1)S(1)}) custom-call(bf16[32,8,1152]{2,1,0:T(8,128)(2,1)S(1)} %all-to-all-done.4.arrived, bf16[2,384,128]{2,1,0:T(8,128)(2,1)S(1)} %bitcast.7, bf16[128,1152]{1,0:T(8,128)(2,1)S(1)} %get-tuple-element.31.normed, f32[128,1152]{1,0:T(8,128)S(1)} %get-tuple-element.43.hat, ...), custom_call_target="tpu_custom_call" | custom-call | tf_op jit(solution)/shard_map/pallas_call | solution.py:132
  99.4 0.8 copy-done.5
  100.2 2.6 %all-to-all-start.6 = ((bf16[32,24,128]{2,1,0:T(8,128)(2,1)}), bf16[32,24,128]{2,1,0:T(8,128)(2,1)S(1)}, u32[]{:S(2)}, u32[]{:S(2)}) async-start(bf16[32,24,128]{2,1,0:T(8,128)(2,1)} %get-tuple-element.47), calls=%async_computation.6 | async-start | bytes 393216 | tf_op jit(solution)/shard_map/all_to_all | solution.py:427
  102.8 0.0 copy-start.6
  102.8 1.0 copy.41
  103.8 0.1 copy-done.6
  103.8 0.3 copy.42
  104.1 8.5 %all-to-all-done.6.arrived = bf16[32,24,128]{2,1,0:T(8,128)(2,1)S(1)} async-done(((bf16[32,24,128]{2,1,0:T(8,128)(2,1)}), bf16[32,24,128]{2,1,0:T(8,128)(2,1)S(1)}, u32[]{:S(2)}, u32[]{:S(2)}) %all-to-all-start.6) | async-done | bytes 196640 | tf_op jit(solution)/shard_map/all_to_all | solution.py:427
  112.6 3.5 %all-to-all-start.2 = ((bf16[2,12,96,64]{2,3,1,0:T(8,128)(2,1)}), bf16[2,12,96,64]{2,3,1,0:T(8,128)(2,1)S(1)}, u32[]{:S(2)}, u32[]{:S(2)}) async-start(bf16[2,12,96,64]{2,3,1,0:T(8,128)(2,1)} %copy.41), calls=%async_computation.2 | async-start | bytes 786432 | tf_op jit(solution)/shard_map/all_to_all | solution.py:413
  116.1 1.6 %all-to-all-done.2 = bf16[2,12,96,64]{2,3,1,0:T(8,128)(2,1)S(1)} async-done(((bf16[2,12,96,64]{2,3,1,0:T(8,128)(2,1)}), bf16[2,12,96,64]{2,3,1,0:T(8,128)(2,1)S(1)}, u32[]{:S(2)}, u32[]{:S(2)}) %all-to-all-start.2) | async-done | bytes 294944 | tf_op jit(solution)/shard_map/all_to_all | solution.py:413
  117.7 4.0 %all_to_all.42 = bf16[2,12,96,64]{2,3,1,0:T(8,128)(2,1)S(1)} all-to-all(bf16[2,12,96,64]{2,3,1,0:T(8,128)(2,1)S(1)} %copy.42), channel_id=1, replica_groups=mesh['row'=8,'col'=2,'ch'=2] {'ch'}, dimensions={0} | all-to-all | bytes 589824 | tf_op jit(solution)/shard_map/all_to_all | solution.py:428
  121.7 0.7 broadcast_in_dim.2
  122.4 3.5 %all-to-all-start.7 = ((bf16[16,24,128]{2,1,0:T(8,128)(2,1)}), bf16[16,24,128]{2,1,0:T(8,128)(2,1)S(1)}, u32[]{:S(2)}, u32[]{:S(2)}) async-start(bf16[16,24,128]{2,1,0:T(8,128)(2,1)} %broadcast_in_dim.2), calls=%async_computation.7 | async-start | bytes 196608 | tf_op jit(solution)/shard_map/all_to_all | solution.py:431
  125.9 7.6 %all-to-all-done.7.sums = bf16[16,24,128]{2,1,0:T(8,128)(2,1)S(1)} async-done(((bf16[16,24,128]{2,1,0:T(8,128)(2,1)}), bf16[16,24,128]{2,1,0:T(8,128)(2,1)S(1)}, u32[]{:S(2)}, u32[]{:S(2)}) %all-to-all-start.7) | async-done | bytes 98336 | tf_op jit(solution)/shard_map/all_to_all | solution.py:431
  133.5 0.4 shard_map.161
  133.9 0.7 copy.43
  134.6 0.7 copy.44
  135.3 0.7 copy.45
  136.0 0.7 copy.46
  136.7 0.7 copy.47
  137.4 0.7 copy.48
  138.1 0.7 copy.51
  138.9 0.7 copy.52
  (7 shorter events, 0.1 us)
Async XLA Ops:
  0.6 5.1 %copy-start.11 = (bf16[128,128]{1,0:T(8,128)(2,1)S(1)}, bf16[128,128]{1,0:T(8,128)(2,1)}, u32[]{:S(2)}) copy-start(bf16[128,128]{1,0:T(8,128)(2,1)} %constant.14.clone.order) | copy-start | bytes 98308
  0.6 7.4 %copy-start.4 = (bf16[24,96,128]{2,1,0:T(8,128)(2,1)S(1)}, bf16[24,96,128]{2,1,0:T(8,128)(2,1)}, u32[]{:S(2)}) copy-start(bf16[24,96,128]{2,1,0:T(8,128)(2,1)} %pair.1) | copy-start | bytes 1769476
  39.5 2.7 %copy-start.12 = (bf16[24,96,64]{1,2,0:T(8,128)(2,1)S(1)}, bf16[24,96,64]{1,2,0:T(8,128)(2,1)}, u32[]{:S(2)}) copy-start(bf16[24,96,64]{1,2,0:T(8,128)(2,1)} %param.10) | copy-start | bytes 884740
  39.5 13.7 %all-to-all-start.1 = ((bf16[32,4,1152]{2,1,0:T(4,128)(2,1)}), bf16[32,4,1152]{2,1,0:T(4,128)(2,1)S(1)}, u32[]{:S(2)}, u32[]{:S(2)}) async-start(bf16[32,4,1152]{2,1,0:T(4,128)(2,1)} %get-tuple-element.33), calls=%async_computation.1 | async-start | bytes 589824 | tf_op jit(solution)/shard_map/all_to_all | solution.py:401
  42.6 1.6 %collective-permute-start = (bf16[12,96,64]{2,1,0:T(8,128)(2,1)S(1)}, bf16[12,96,64]{2,1,0:T(8,128)(2,1)S(1)}, u32[]{:S(2)}, u32[]{:S(2)}) collective-permute-start(bf16[12,96,64]{2,1,0:T(8,128)(2,1)S(1)} %constant_dynamic-slice_fusion), channel_id=1, source_target_pairs={{0,1},{1,0},{2,3},{3,2},{4,5},{5,4},{6,7},{7,6},{8,9},{9,8},{10,11... | collective-permute-start | bytes 442376 | tf_op jit(solution)/shard_map/ppermute | solution.py:377
  44.5 0.8 copy-start
  45.4 0.8 copy-start.2
  53.3 1.1 copy-start.1
  54.3 1.1 copy-start.3
  56.1 0.7 copy-start.7
  56.8 0.7 copy-start.9
  77.1 2.8 %copy-start.8 = (bf16[128,1152]{1,0:T(8,128)(2,1)S(1)}, bf16[128,1152]{1,0:T(8,128)(2,1)}, u32[]{:S(2)}) copy-start(bf16[128,1152]{1,0:T(8,128)(2,1)} %copy-done.7) | copy-start | bytes 884740
  77.1 20.1 %all-to-all-start.4 = ((bf16[32,8,1152]{2,1,0:T(8,128)(2,1)}), bf16[32,8,1152]{2,1,0:T(8,128)(2,1)S(1)}, u32[]{:S(2)}, u32[]{:S(2)}) async-start(bf16[32,8,1152]{2,1,0:T(8,128)(2,1)} %shard_map.158), calls=%async_computation.4 | async-start | bytes 1179648 | tf_op jit(solution)/shard_map/all_to_all | solution.py:420
  79.9 1.0 copy-start.10
  99.4 0.8 copy-start.5
  100.2 12.4 %all-to-all-start.6 = ((bf16[32,24,128]{2,1,0:T(8,128)(2,1)}), bf16[32,24,128]{2,1,0:T(8,128)(2,1)S(1)}, u32[]{:S(2)}, u32[]{:S(2)}) async-start(bf16[32,24,128]{2,1,0:T(8,128)(2,1)} %get-tuple-element.47), calls=%async_computation.6 | async-start | bytes 393216 | tf_op jit(solution)/shard_map/all_to_all | solution.py:427
  102.8 1.1 copy-start.6
  112.6 5.1 %all-to-all-start.2 = ((bf16[2,12,96,64]{2,3,1,0:T(8,128)(2,1)}), bf16[2,12,96,64]{2,3,1,0:T(8,128)(2,1)S(1)}, u32[]{:S(2)}, u32[]{:S(2)}) async-start(bf16[2,12,96,64]{2,3,1,0:T(8,128)(2,1)} %copy.41), calls=%async_computation.2 | async-start | bytes 786432 | tf_op jit(solution)/shard_map/all_to_all | solution.py:413
  122.4 11.1 %all-to-all-start.7 = ((bf16[16,24,128]{2,1,0:T(8,128)(2,1)}), bf16[16,24,128]{2,1,0:T(8,128)(2,1)S(1)}, u32[]{:S(2)}, u32[]{:S(2)}) async-start(bf16[16,24,128]{2,1,0:T(8,128)(2,1)} %broadcast_in_dim.2), calls=%async_computation.7 | async-start | bytes 196608 | tf_op jit(solution)/shard_map/all_to_all | solution.py:431
